TPU v7x, 512 devices: a whole 4x4x16 slice. The times are simulated.
512 devices in a mesh: net: 64 (over z, x), scen: 8 (over y, core).
Axes of the slice: x: 4, y: 4, z: 16, core: 2. Of those that a mesh axis runs over, the one named last changes fastest.
Arguments:
- device_group: int32 [64], replicated, may hold values from 3 to 63, as said below
- column_blocks: int32 [256, 12], P('net'), may hold values from 0 to 255, as said below
- impedance_real: bfloat16 [256, 12, 128, 128], P('net'), may hold values from 0 to 0.015258789
- impedance_imag: bfloat16 [256, 12, 128, 128], P('net'), may hold values from 0 to 0.0076293945
- building_phase: int32 [65536], P('net'), may hold values from 0 to 32767, as said below
- building_power: float32 [65536], P('net'), may hold values from 0.2 to 1
- reactive_ratio: float32 [65536], P('net'), may hold values from 0.1 to 0.8
- copula_normals: float32 [65536, 1024], P('net', 'scen'), may hold values from -6 to 6
- source_angle: float32 [32768], P('net'), may hold values from -3.140625 to 3.140625
Outputs:
- voltage_real: float32 [32768, 1024], P('net', 'scen')
- voltage_imag: float32 [32768, 1024], P('net', 'scen')
- drop_mean: float32 [32768, 16], P('net')
Inputs may be any that keep to these rules, and one draw needn't show every extreme that they name: `device_group`: never falling along the devices; each group is a run of 1 to 4 consecutive devices and is labelled by the index of its last device; the first 4 devices form one group. `column_blocks`: slot 0 of block row r is r itself; the first min(12, 4 times the devices of r's group) slots are distinct blocks of devices of r's group; the other slots repeat r. `building_phase`: building b feeds a phase of the device that holds b: from 512 * (b // 1024) to that plus 512 - 1; every phase is fed by at least one building.
All inputs are finite; a program needn't handle non-finite values.
Results may differ from a plain program's by a relative error of at most 0.0063.
Values may be sent and summed in bfloat16 or wider, within the bound.
No kernel may reach another device: no remote copies, remote signals or barrier semaphores. Data moves between devices by JAX's collectives and lax.ppermute only.
A program may use at most 64 MiB of HBM per device.

v0:
```python
import jax
import jax.numpy as jnp
from jax import lax
from jax.sharding import PartitionSpec as P

GMAX = 4
ITERS = 3
TIMES = 16
floor_square = 0.49


def from_behind(value, axis, steps):
    count = lax.axis_size(axis)
    leading, last = (max(0, -steps), min(count, count - steps))
    return lax.ppermute(value, axis, [(source, source + steps) for source in range(leading, last)])


def shards(
    device_group,
    column_blocks,
    impedance_real,
    impedance_imag,
    building_phase,
    building_power,
    reactive_ratio,
    copula_normals,
    source_angle,
):
    block_count, slot_count, block_width, other_width = impedance_real.shape
    phase_count = block_count * block_width
    column_count = copula_normals.shape[1]
    local_scen = column_count // TIMES
    total_scen = local_scen * lax.axis_size("scen")
    scenario = (
        lax.axis_index("scen") * local_scen + jnp.arange(column_count, dtype=jnp.int32) // TIMES
    ).astype(jnp.float32)
    scen_level = 0.5 + scenario / (total_scen - 1)
    real_power = (
        building_power[:, None] * scen_level[None, :] * jnp.exp(0.4 * copula_normals - 0.08)
    )
    both_power = jnp.concatenate([real_power, real_power * reactive_ratio[:, None]], axis=1)
    net_index = lax.axis_index("net")
    local_phase = building_phase - net_index * phase_count
    loads = jax.ops.segment_sum(both_power, local_phase, num_segments=phase_count)
    load_real = loads[:, :column_count]
    load_reactive = loads[:, column_count:]
    source_real = jnp.broadcast_to(jnp.cos(source_angle)[:, None], (phase_count, column_count))
    source_imag = jnp.broadcast_to(jnp.sin(source_angle)[:, None], (phase_count, column_count))
    own_group = device_group[net_index]
    group_size = jnp.sum((device_group == own_group).astype(jnp.int32))
    live_count = jnp.minimum(slot_count, group_size * block_count)
    live_slots = jnp.arange(slot_count, dtype=jnp.int32) < live_count
    owner_device = column_blocks // block_count
    window_index = (
        owner_device - net_index + (GMAX - 1)
    ) * block_count + column_blocks % block_count
    volt_real = source_real
    volt_imag = source_imag
    for sweep in range(ITERS):
        mag_square = jnp.maximum(volt_real * volt_real + volt_imag * volt_imag, floor_square)
        current_real = (load_real * volt_real + load_reactive * volt_imag) / mag_square
        current_imag = (load_real * volt_imag - load_reactive * volt_real) / mag_square
        currents = jnp.concatenate([current_real, current_imag], axis=1).astype(jnp.bfloat16)
        lower_parts = []
        upper_parts = []
        for distance in range(1, GMAX):
            lower_parts.append(from_behind(currents, "net", distance))
            upper_parts.append(from_behind(currents, "net", -distance))
        nearby = jnp.concatenate(lower_parts[::-1] + [currents] + upper_parts, axis=0).reshape(
            -1, block_width, 2 * column_count
        )
        gathered = jnp.take(nearby, window_index, axis=0)
        gathered = jnp.where(live_slots[None, :, None, None], gathered, jnp.zeros((), jnp.bfloat16))
        real_part = jnp.einsum(
            "bsij,bsjk->bik", impedance_real, gathered, preferred_element_type=jnp.float32
        ).reshape(phase_count, 2 * column_count)
        imag_part = jnp.einsum(
            "bsij,bsjk->bik", impedance_imag, gathered, preferred_element_type=jnp.float32
        ).reshape(phase_count, 2 * column_count)
        drop_real = real_part[:, :column_count] - imag_part[:, column_count:]
        drop_imag = real_part[:, column_count:] + imag_part[:, :column_count]
        volt_real = source_real - drop_real
        volt_imag = source_imag - drop_imag
    magnitude = jnp.sqrt(volt_real * volt_real + volt_imag * volt_imag)
    local_sum = jnp.sum(magnitude.reshape(phase_count, local_scen, TIMES), axis=1)
    scen_total = lax.psum(local_sum, "scen")
    drop_mean = 100.0 * (1.0 - scen_total / total_scen)
    return (volt_real, volt_imag, drop_mean)


def solution(mesh):
    in_specs = (
        P(),
        P("net", None),
        P("net", None, None, None),
        P("net", None, None, None),
        P("net"),
        P("net"),
        P("net"),
        P("net", "scen"),
        P("net"),
    )
    out_specs = (P("net", "scen"), P("net", "scen"), P("net", None))
    return jax.shard_map(shards, mesh=mesh, in_specs=in_specs, out_specs=out_specs, check_vma=False)
```

profile of v0, /device:TPU:224, one launch (start us, length us, event | category | flops | bytes accessed | tf_op | source)
XLA Modules:
  0.0 170.0 jit_solution(13973513056029608391)
XLA Ops:
  0.7 0.8 fusion.42
  1.5 0.7 broadcast_subtract_fusion
  2.2 1.4 broadcast_multiply_fusion
  3.6 6.2 %scatter_custom_fusion = f32[512,256]{1,0:T(8,128)S(1)} fusion(s32[1024]{0:T(1024)S(1)} %broadcast_subtract_fusion, f32[1024,128]{1,0:T(8,128)S(1)} %get-tuple-element.12, f32[]{:T(128)} %constant.112, f32[1024,128]{1,0:T(8,128)S(1)} %get-tuple-element.13, f32[]{:T(128)} %constant.78.clone.1), kind=kCustom, calls=%fused_computation.7 | custom fusion | flops 524288 | bytes 1572872 | tf_op jit(solution)/shard_map/scatter-add | solution.py:44
  9.9 0.3 divide_convert_fusion.5
  10.2 4.7 %collective-permute-start = (bf16[512,256]{1,0:T(8,128)(2,1)S(1)}, bf16[512,256]{1,0:T(8,128)(2,1)}, u32[]{:S(2)}, u32[]{:S(2)}) collective-permute-start(bf16[512,256]{1,0:T(8,128)(2,1)S(1)} %pad_maximum_fusion), channel_id=1, source_target_pairs={{0,24},{8,32},{16,40},{24,48},{32,56},{40,64},{48,72},{56,80},{64,... | collective-permute-start | bytes 786440 | tf_op jit(solution)/shard_map/ppermute | solution.py:15
  14.9 5.3 %collective-permute-start.1 = (bf16[512,256]{1,0:T(8,128)(2,1)S(1)}, bf16[512,256]{1,0:T(8,128)(2,1)}, u32[]{:S(2)}, u32[]{:S(2)}) collective-permute-start(bf16[512,256]{1,0:T(8,128)(2,1)S(1)} %pad_maximum_fusion), channel_id=1, source_target_pairs={{0,16},{8,24},{16,32},{24,40},{32,48},{40,56},{48,64},{56,72},{64,... | collective-permute-start | bytes 786440 | tf_op jit(solution)/shard_map/ppermute | solution.py:15
  20.1 2.8 %collective-permute-start.2 = (bf16[512,256]{1,0:T(8,128)(2,1)S(1)}, bf16[512,256]{1,0:T(8,128)(2,1)S(1)}, u32[]{:S(2)}, u32[]{:S(2)}) collective-permute-start(bf16[512,256]{1,0:T(8,128)(2,1)S(1)} %pad_maximum_fusion), channel_id=1, source_target_pairs={{0,8},{8,16},{16,24},{24,32},{32,40},{40,48},{48,56},{56,64},{64,7... | collective-permute-start | bytes 786440 | tf_op jit(solution)/shard_map/ppermute | solution.py:15
  22.9 5.2 %collective-permute-start.3 = (bf16[512,256]{1,0:T(8,128)(2,1)S(1)}, bf16[512,256]{1,0:T(8,128)(2,1)S(1)}, u32[]{:S(2)}, u32[]{:S(2)}) collective-permute-start(bf16[512,256]{1,0:T(8,128)(2,1)S(1)} %pad_maximum_fusion), channel_id=1, source_target_pairs={{8,0},{16,8},{24,16},{32,24},{40,32},{48,40},{56,48},{64,56},{72,6... | collective-permute-start | bytes 786440 | tf_op jit(solution)/shard_map/ppermute | solution.py:15
  28.1 1.9 %collective-permute-start.4 = (bf16[512,256]{1,0:T(8,128)(2,1)S(1)}, bf16[512,256]{1,0:T(8,128)(2,1)S(1)}, u32[]{:S(2)}, u32[]{:S(2)}) collective-permute-start(bf16[512,256]{1,0:T(8,128)(2,1)S(1)} %pad_maximum_fusion), channel_id=1, source_target_pairs={{16,0},{24,8},{32,16},{40,24},{48,32},{56,40},{64,48},{72,56},{80,... | collective-permute-start | bytes 786440 | tf_op jit(solution)/shard_map/ppermute | solution.py:15
  30.1 0.1 reshape.115
  30.2 0.6 dynamic_slice.3
  30.7 1.3 fusion.27
  32.7 1.9 %collective-permute-start.5 = (bf16[512,256]{1,0:T(8,128)(2,1)S(1)}, bf16[512,256]{1,0:T(8,128)(2,1)S(1)}, u32[]{:S(2)}, u32[]{:S(2)}) collective-permute-start(bf16[512,256]{1,0:T(8,128)(2,1)S(1)} %pad_maximum_fusion), channel_id=1, source_target_pairs={{24,0},{32,8},{40,16},{48,24},{56,32},{64,40},{72,48},{80,56},{88,... | collective-permute-start | bytes 786440 | tf_op jit(solution)/shard_map/ppermute | solution.py:15
  34.6 1.7 constant_dynamic-update-slice_fusion.6
  36.3 1.7 constant_dynamic-update-slice_fusion.5
  38.0 0.7 constant_dynamic-update-slice_fusion.4
  38.7 0.7 constant_dynamic-update-slice_fusion.3
  39.4 0.7 constant_dynamic-update-slice_fusion.2
  40.2 5.0 %collective-permute-done.4 = bf16[512,256]{1,0:T(8,128)(2,1)S(1)} collective-permute-done((bf16[512,256]{1,0:T(8,128)(2,1)S(1)}, bf16[512,256]{1,0:T(8,128)(2,1)S(1)}, u32[]{:S(2)}, u32[]{:S(2)}) %collective-permute-start.4) | collective-permute-done | bytes 262176 | tf_op jit(solution)/shard_map/ppermute | solution.py:15
  45.2 0.7 constant_dynamic-update-slice_fusion.1
  45.9 0.7 constant_dynamic-update-slice_fusion
  46.7 4.0 %gather_fusion = bf16[48,128,256]{2,1,0:T(8,128)(2,1)} fusion(bf16[28,128,256]{2,1,0:T(8,128)(2,1)} %bitcast.1, s32[1024]{0:T(1024)S(1)} %pad_clamp_fusion), kind=kCustom, calls=%fused_computation.clone | custom fusion | bytes 6291648 | tf_op jit(solution)/shard_map/jit(_take)/gather | solution.py:72
  50.7 2.8 %fusion.4 = f32[4,256,128,1]{1,2,3,0:T(8,128)S(1)} fusion(bf16[4,12,128,128]{3,2,1,0:T(8,128)(2,1)S(1)} %copy-done, bf16[4,12,128,256]{3,2,1,0:T(8,128)(2,1)} %bitcast.53, pred[12]{0:T(512)(128)(4,1)S(1)} %iota_compare_fusion, pred[4,12]{1,0:T(4,128)(4,1)S(1)} %get-tuple-element.10), kind=kOutput, calls=%fused_computation.11 | convolution fusion | flops 405798912 | bytes 5242940 | tf_op jit(solution)/shard_map/bsij,bsjk->bik/dot_general | solution.py:74
  53.5 0.4 copy-done.5
  54.0 0.8 fusion.5
  54.8 0.2 divide_convert_fusion.3
  55.0 1.9 %collective-permute-start.6 = (bf16[512,256]{1,0:T(8,128)(2,1)S(1)}, bf16[512,256]{1,0:T(8,128)(2,1)S(1)}, u32[]{:S(2)}, u32[]{:S(2)}) collective-permute-start(bf16[512,256]{1,0:T(8,128)(2,1)S(1)} %pad_maximum_fusion.1), channel_id=1, source_target_pairs={{0,24},{8,32},{16,40},{24,48},{32,56},{40,64},{48,72},{56,80},{64,... | collective-permute-start | bytes 786440 | tf_op jit(solution)/shard_map/ppermute | solution.py:15
  57.0 10.6 %collective-permute-start.7 = (bf16[512,256]{1,0:T(8,128)(2,1)S(1)}, bf16[512,256]{1,0:T(8,128)(2,1)S(1)}, u32[]{:S(2)}, u32[]{:S(2)}) collective-permute-start(bf16[512,256]{1,0:T(8,128)(2,1)S(1)} %pad_maximum_fusion.1), channel_id=1, source_target_pairs={{0,16},{8,24},{16,32},{24,40},{32,48},{40,56},{48,64},{56,72},{64,... | collective-permute-start | bytes 786440 | tf_op jit(solution)/shard_map/ppermute | solution.py:15
  67.6 1.9 %collective-permute-start.8 = (bf16[512,256]{1,0:T(8,128)(2,1)S(1)}, bf16[512,256]{1,0:T(8,128)(2,1)S(1)}, u32[]{:S(2)}, u32[]{:S(2)}) collective-permute-start(bf16[512,256]{1,0:T(8,128)(2,1)S(1)} %pad_maximum_fusion.1), channel_id=1, source_target_pairs={{0,8},{8,16},{16,24},{24,32},{32,40},{40,48},{48,56},{56,64},{64,7... | collective-permute-start | bytes 786440 | tf_op jit(solution)/shard_map/ppermute | solution.py:15
  69.5 6.0 %collective-permute-start.9 = (bf16[512,256]{1,0:T(8,128)(2,1)S(1)}, bf16[512,256]{1,0:T(8,128)(2,1)S(1)}, u32[]{:S(2)}, u32[]{:S(2)}) collective-permute-start(bf16[512,256]{1,0:T(8,128)(2,1)S(1)} %pad_maximum_fusion.1), channel_id=1, source_target_pairs={{8,0},{16,8},{24,16},{32,24},{40,32},{48,40},{56,48},{64,56},{72,6... | collective-permute-start | bytes 786440 | tf_op jit(solution)/shard_map/ppermute | solution.py:15
  75.5 1.9 %collective-permute-start.10 = (bf16[512,256]{1,0:T(8,128)(2,1)S(1)}, bf16[512,256]{1,0:T(8,128)(2,1)S(1)}, u32[]{:S(2)}, u32[]{:S(2)}) collective-permute-start(bf16[512,256]{1,0:T(8,128)(2,1)S(1)} %pad_maximum_fusion.1), channel_id=1, source_target_pairs={{16,0},{24,8},{32,16},{40,24},{48,32},{56,40},{64,48},{72,56},{80,... | collective-permute-start | bytes 786440 | tf_op jit(solution)/shard_map/ppermute | solution.py:15
  77.5 1.9 %collective-permute-start.11 = (bf16[512,256]{1,0:T(8,128)(2,1)S(1)}, bf16[512,256]{1,0:T(8,128)(2,1)S(1)}, u32[]{:S(2)}, u32[]{:S(2)}) collective-permute-start(bf16[512,256]{1,0:T(8,128)(2,1)S(1)} %pad_maximum_fusion.1), channel_id=1, source_target_pairs={{24,0},{32,8},{40,16},{48,24},{56,32},{64,40},{72,48},{80,56},{88,... | collective-permute-start | bytes 786440 | tf_op jit(solution)/shard_map/ppermute | solution.py:15
  79.4 0.7 constant_dynamic-update-slice_fusion.13
  80.1 0.7 constant_dynamic-update-slice_fusion.12
  80.8 0.7 constant_dynamic-update-slice_fusion.11
  81.6 0.7 constant_dynamic-update-slice_fusion.10
  82.3 0.0 collective-permute-done.9
  82.3 0.7 constant_dynamic-update-slice_fusion.9
  83.1 7.1 %collective-permute-done.10 = bf16[512,256]{1,0:T(8,128)(2,1)S(1)} collective-permute-done((bf16[512,256]{1,0:T(8,128)(2,1)S(1)}, bf16[512,256]{1,0:T(8,128)(2,1)S(1)}, u32[]{:S(2)}, u32[]{:S(2)}) %collective-permute-start.10) | collective-permute-done | bytes 262176 | tf_op jit(solution)/shard_map/ppermute | solution.py:15
  90.2 0.7 constant_dynamic-update-slice_fusion.8
  90.9 0.7 constant_dynamic-update-slice_fusion.7
  91.7 4.0 %gather_fusion.1 = bf16[48,128,256]{2,1,0:T(8,128)(2,1)} fusion(bf16[28,128,256]{2,1,0:T(8,128)(2,1)} %bitcast.15, s32[1024]{0:T(1024)S(1)} %pad_clamp_fusion), kind=kCustom, calls=%fused_computation.1.clone | custom fusion | bytes 6291648 | tf_op jit(solution)/shard_map/jit(_take)/gather | solution.py:72
  95.7 2.8 %fusion.6 = f32[4,256,128,1]{1,2,3,0:T(8,128)S(1)} fusion(bf16[4,12,128,128]{3,2,1,0:T(8,128)(2,1)S(1)} %copy-done, bf16[4,12,128,256]{3,2,1,0:T(8,128)(2,1)} %bitcast.55, pred[12]{0:T(512)(128)(4,1)S(1)} %iota_compare_fusion, pred[4,12]{1,0:T(4,128)(4,1)S(1)} %get-tuple-element.10), kind=kOutput, calls=%fused_computation.13 | convolution fusion | flops 405798912 | bytes 5242940 | tf_op jit(solution)/shard_map/bsij,bsjk->bik/dot_general | solution.py:74
  98.5 0.4 copy-done.6
  99.0 0.8 fusion.7
  99.8 0.2 divide_convert_fusion.1
  100.1 1.9 %collective-permute-start.12 = (bf16[512,256]{1,0:T(8,128)(2,1)S(1)}, bf16[512,256]{1,0:T(8,128)(2,1)S(1)}, u32[]{:S(2)}, u32[]{:S(2)}) collective-permute-start(bf16[512,256]{1,0:T(8,128)(2,1)S(1)} %pad_maximum_fusion.2), channel_id=1, source_target_pairs={{0,24},{8,32},{16,40},{24,48},{32,56},{40,64},{48,72},{56,80},{64,... | collective-permute-start | bytes 786440 | tf_op jit(solution)/shard_map/ppermute | solution.py:15
  102.0 5.8 %collective-permute-start.13 = (bf16[512,256]{1,0:T(8,128)(2,1)S(1)}, bf16[512,256]{1,0:T(8,128)(2,1)S(1)}, u32[]{:S(2)}, u32[]{:S(2)}) collective-permute-start(bf16[512,256]{1,0:T(8,128)(2,1)S(1)} %pad_maximum_fusion.2), channel_id=1, source_target_pairs={{0,16},{8,24},{16,32},{24,40},{32,48},{40,56},{48,64},{56,72},{64,... | collective-permute-start | bytes 786440 | tf_op jit(solution)/shard_map/ppermute | solution.py:15
  107.8 3.5 %collective-permute-start.14 = (bf16[512,256]{1,0:T(8,128)(2,1)S(1)}, bf16[512,256]{1,0:T(8,128)(2,1)S(1)}, u32[]{:S(2)}, u32[]{:S(2)}) collective-permute-start(bf16[512,256]{1,0:T(8,128)(2,1)S(1)} %pad_maximum_fusion.2), channel_id=1, source_target_pairs={{0,8},{8,16},{16,24},{24,32},{32,40},{40,48},{48,56},{56,64},{64,7... | collective-permute-start | bytes 786440 | tf_op jit(solution)/shard_map/ppermute | solution.py:15
  111.3 5.5 %collective-permute-start.15 = (bf16[512,256]{1,0:T(8,128)(2,1)S(1)}, bf16[512,256]{1,0:T(8,128)(2,1)S(1)}, u32[]{:S(2)}, u32[]{:S(2)}) collective-permute-start(bf16[512,256]{1,0:T(8,128)(2,1)S(1)} %pad_maximum_fusion.2), channel_id=1, source_target_pairs={{8,0},{16,8},{24,16},{32,24},{40,32},{48,40},{56,48},{64,56},{72,6... | collective-permute-start | bytes 786440 | tf_op jit(solution)/shard_map/ppermute | solution.py:15
  116.8 3.4 %collective-permute-start.16 = (bf16[512,256]{1,0:T(8,128)(2,1)S(1)}, bf16[512,256]{1,0:T(8,128)(2,1)S(1)}, u32[]{:S(2)}, u32[]{:S(2)}) collective-permute-start(bf16[512,256]{1,0:T(8,128)(2,1)S(1)} %pad_maximum_fusion.2), channel_id=1, source_target_pairs={{16,0},{24,8},{32,16},{40,24},{48,32},{56,40},{64,48},{72,56},{80,... | collective-permute-start | bytes 786440 | tf_op jit(solution)/shard_map/ppermute | solution.py:15
  120.2 1.9 %collective-permute-start.17 = (bf16[512,256]{1,0:T(8,128)(2,1)S(1)}, bf16[512,256]{1,0:T(8,128)(2,1)S(1)}, u32[]{:S(2)}, u32[]{:S(2)}) collective-permute-start(bf16[512,256]{1,0:T(8,128)(2,1)S(1)} %pad_maximum_fusion.2), channel_id=1, source_target_pairs={{24,0},{32,8},{40,16},{48,24},{56,32},{64,40},{72,48},{80,56},{88,... | collective-permute-start | bytes 786440 | tf_op jit(solution)/shard_map/ppermute | solution.py:15
  122.2 4.5 %collective-permute-done.14 = bf16[512,256]{1,0:T(8,128)(2,1)S(1)} collective-permute-done((bf16[512,256]{1,0:T(8,128)(2,1)S(1)}, bf16[512,256]{1,0:T(8,128)(2,1)S(1)}, u32[]{:S(2)}, u32[]{:S(2)}) %collective-permute-start.14) | collective-permute-done | bytes 262176 | tf_op jit(solution)/shard_map/ppermute | solution.py:15
  126.7 7.5 %collective-permute-done.16 = bf16[512,256]{1,0:T(8,128)(2,1)S(1)} collective-permute-done((bf16[512,256]{1,0:T(8,128)(2,1)S(1)}, bf16[512,256]{1,0:T(8,128)(2,1)S(1)}, u32[]{:S(2)}, u32[]{:S(2)}) %collective-permute-start.16) | collective-permute-done | bytes 262176 | tf_op jit(solution)/shard_map/ppermute | solution.py:15
  134.2 1.5 collective-permute-done.17
  135.8 2.5 %gather_fusion.2 = bf16[48,128,256]{2,1,0:T(8,128)(2,1)} fusion(bf16[28,128,256]{2,1,0:T(8,128)(2,1)S(1)} %bitcast.50, s32[1024]{0:T(1024)S(1)} %pad_clamp_fusion), kind=kCustom, calls=%fused_computation.2.clone | custom fusion | bytes 6291648 | tf_op jit(solution)/shard_map/jit(_take)/gather | solution.py:72
  138.3 2.8 %fusion.8 = f32[4,256,128,1]{1,2,3,0:T(8,128)S(1)} fusion(bf16[4,12,128,128]{3,2,1,0:T(8,128)(2,1)S(1)} %copy-done, bf16[4,12,128,256]{3,2,1,0:T(8,128)(2,1)} %bitcast.51, pred[12]{0:T(512)(128)(4,1)S(1)} %iota_compare_fusion, pred[4,12]{1,0:T(4,128)(4,1)S(1)} %get-tuple-element.10), kind=kOutput, calls=%fused_computation.15 | convolution fusion | flops 405798912 | bytes 5242940 | tf_op jit(solution)/shard_map/bsij,bsjk->bik/dot_general | solution.py:74
  141.2 0.4 copy-done.7
  141.6 0.8 fusion.9
  142.4 1.0 add_sqrt_fusion
  143.4 0.1 copy.30
  143.6 25.8 %psum.7 = f32[512,16]{0,1:T(8,128)S(1)} all-reduce(f32[512,16]{0,1:T(8,128)S(1)} %reduce_sum.19), channel_id=1, replica_groups=mesh['net'=64,'scen'=8] {'scen'}, use_global_device_ids=true, to_apply=%region_3.5 | all-reduce | flops 8192 | bytes 65536 | tf_op jit(solution)/shard_map/psum | solution.py:86
  169.4 0.6 subtract_multiply_fusion
  (43 shorter events, 0.4 us)
Async XLA Ops:
  0.6 50.0 %copy-start = (bf16[4,12,128,128]{3,2,1,0:T(8,128)(2,1)S(1)}, bf16[4,12,128,128]{3,2,1,0:T(8,128)(2,1)}, u32[]{:S(2)}) copy-start(bf16[4,12,128,128]{3,2,1,0:T(8,128)(2,1)} %param.13) | copy-start | bytes 4718596
  3.6 26.5 %copy-start.4 = (s32[4,12]{1,0:T(4,128)S(1)}, s32[4,12]{1,0:T(4,128)}, u32[]{:S(2)}) copy-start(s32[4,12]{1,0:T(4,128)} %param.12) | copy-start | bytes 580
  3.6 26.6 %copy-start.8 = (s32[64]{0:T(128)S(1)}, s32[64]{0:T(128)}, u32[]{:S(2)}) copy-start(s32[64]{0:T(128)} %param.11) | copy-start | bytes 772
  10.2 22.5 %collective-permute-start = (bf16[512,256]{1,0:T(8,128)(2,1)S(1)}, bf16[512,256]{1,0:T(8,128)(2,1)}, u32[]{:S(2)}, u32[]{:S(2)}) collective-permute-start(bf16[512,256]{1,0:T(8,128)(2,1)S(1)} %pad_maximum_fusion), channel_id=1, source_target_pairs={{0,24},{8,32},{16,40},{24,48},{32,56},{40,64},{48,72},{56,80},{64,... | collective-permute-start | bytes 786440 | tf_op jit(solution)/shard_map/ppermute | solution.py:15
  14.9 21.4 %collective-permute-start.1 = (bf16[512,256]{1,0:T(8,128)(2,1)S(1)}, bf16[512,256]{1,0:T(8,128)(2,1)}, u32[]{:S(2)}, u32[]{:S(2)}) collective-permute-start(bf16[512,256]{1,0:T(8,128)(2,1)S(1)} %pad_maximum_fusion), channel_id=1, source_target_pairs={{0,16},{8,24},{16,32},{24,40},{32,48},{40,56},{48,64},{56,72},{64,... | collective-permute-start | bytes 786440 | tf_op jit(solution)/shard_map/ppermute | solution.py:15
  20.1 17.8 %collective-permute-start.2 = (bf16[512,256]{1,0:T(8,128)(2,1)S(1)}, bf16[512,256]{1,0:T(8,128)(2,1)S(1)}, u32[]{:S(2)}, u32[]{:S(2)}) collective-permute-start(bf16[512,256]{1,0:T(8,128)(2,1)S(1)} %pad_maximum_fusion), channel_id=1, source_target_pairs={{0,8},{8,16},{16,24},{24,32},{32,40},{40,48},{48,56},{56,64},{64,7... | collective-permute-start | bytes 786440 | tf_op jit(solution)/shard_map/ppermute | solution.py:15
  22.9 16.5 %collective-permute-start.3 = (bf16[512,256]{1,0:T(8,128)(2,1)S(1)}, bf16[512,256]{1,0:T(8,128)(2,1)S(1)}, u32[]{:S(2)}, u32[]{:S(2)}) collective-permute-start(bf16[512,256]{1,0:T(8,128)(2,1)S(1)} %pad_maximum_fusion), channel_id=1, source_target_pairs={{8,0},{16,8},{24,16},{32,24},{40,32},{48,40},{56,48},{64,56},{72,6... | collective-permute-start | bytes 786440 | tf_op jit(solution)/shard_map/ppermute | solution.py:15
  28.1 17.1 %collective-permute-start.4 = (bf16[512,256]{1,0:T(8,128)(2,1)S(1)}, bf16[512,256]{1,0:T(8,128)(2,1)S(1)}, u32[]{:S(2)}, u32[]{:S(2)}) collective-permute-start(bf16[512,256]{1,0:T(8,128)(2,1)S(1)} %pad_maximum_fusion), channel_id=1, source_target_pairs={{16,0},{24,8},{32,16},{40,24},{48,32},{56,40},{64,48},{72,56},{80,... | collective-permute-start | bytes 786440 | tf_op jit(solution)/shard_map/ppermute | solution.py:15
  32.7 13.2 %collective-permute-start.5 = (bf16[512,256]{1,0:T(8,128)(2,1)S(1)}, bf16[512,256]{1,0:T(8,128)(2,1)S(1)}, u32[]{:S(2)}, u32[]{:S(2)}) collective-permute-start(bf16[512,256]{1,0:T(8,128)(2,1)S(1)} %pad_maximum_fusion), channel_id=1, source_target_pairs={{24,0},{32,8},{40,16},{48,24},{56,32},{64,40},{72,48},{80,56},{88,... | collective-permute-start | bytes 786440 | tf_op jit(solution)/shard_map/ppermute | solution.py:15
  50.7 2.9 %copy-start.2 = (bf16[48,128,256]{2,1,0:T(8,128)(2,1)S(1)}, bf16[48,128,256]{2,1,0:T(8,128)(2,1)}, u32[]{:S(2)}) copy-start(bf16[48,128,256]{2,1,0:T(8,128)(2,1)} %gather_fusion) | copy-start | bytes 9437188
  50.7 3.3 %copy-start.5 = (bf16[4,12,128,128]{3,2,1,0:T(8,128)(2,1)S(1)}, bf16[4,12,128,128]{3,2,1,0:T(8,128)(2,1)}, u32[]{:S(2)}) copy-start(bf16[4,12,128,128]{3,2,1,0:T(8,128)(2,1)} %param.14) | copy-start | bytes 4718596
  55.0 22.4 %collective-permute-start.6 = (bf16[512,256]{1,0:T(8,128)(2,1)S(1)}, bf16[512,256]{1,0:T(8,128)(2,1)S(1)}, u32[]{:S(2)}, u32[]{:S(2)}) collective-permute-start(bf16[512,256]{1,0:T(8,128)(2,1)S(1)} %pad_maximum_fusion.1), channel_id=1, source_target_pairs={{0,24},{8,32},{16,40},{24,48},{32,56},{40,64},{48,72},{56,80},{64,... | collective-permute-start | bytes 786440 | tf_op jit(solution)/shard_map/ppermute | solution.py:15
  57.0 23.1 %collective-permute-start.7 = (bf16[512,256]{1,0:T(8,128)(2,1)S(1)}, bf16[512,256]{1,0:T(8,128)(2,1)S(1)}, u32[]{:S(2)}, u32[]{:S(2)}) collective-permute-start(bf16[512,256]{1,0:T(8,128)(2,1)S(1)} %pad_maximum_fusion.1), channel_id=1, source_target_pairs={{0,16},{8,24},{16,32},{24,40},{32,48},{40,56},{48,64},{56,72},{64,... | collective-permute-start | bytes 786440 | tf_op jit(solution)/shard_map/ppermute | solution.py:15
  67.6 13.3 %collective-permute-start.8 = (bf16[512,256]{1,0:T(8,128)(2,1)S(1)}, bf16[512,256]{1,0:T(8,128)(2,1)S(1)}, u32[]{:S(2)}, u32[]{:S(2)}) collective-permute-start(bf16[512,256]{1,0:T(8,128)(2,1)S(1)} %pad_maximum_fusion.1), channel_id=1, source_target_pairs={{0,8},{8,16},{16,24},{24,32},{32,40},{40,48},{48,56},{56,64},{64,7... | collective-permute-start | bytes 786440 | tf_op jit(solution)/shard_map/ppermute | solution.py:15
  69.5 12.8 %collective-permute-start.9 = (bf16[512,256]{1,0:T(8,128)(2,1)S(1)}, bf16[512,256]{1,0:T(8,128)(2,1)S(1)}, u32[]{:S(2)}, u32[]{:S(2)}) collective-permute-start(bf16[512,256]{1,0:T(8,128)(2,1)S(1)} %pad_maximum_fusion.1), channel_id=1, source_target_pairs={{8,0},{16,8},{24,16},{32,24},{40,32},{48,40},{56,48},{64,56},{72,6... | collective-permute-start | bytes 786440 | tf_op jit(solution)/shard_map/ppermute | solution.py:15
  75.5 14.6 %collective-permute-start.10 = (bf16[512,256]{1,0:T(8,128)(2,1)S(1)}, bf16[512,256]{1,0:T(8,128)(2,1)S(1)}, u32[]{:S(2)}, u32[]{:S(2)}) collective-permute-start(bf16[512,256]{1,0:T(8,128)(2,1)S(1)} %pad_maximum_fusion.1), channel_id=1, source_target_pairs={{16,0},{24,8},{32,16},{40,24},{48,32},{56,40},{64,48},{72,56},{80,... | collective-permute-start | bytes 786440 | tf_op jit(solution)/shard_map/ppermute | solution.py:15
  77.5 13.5 %collective-permute-start.11 = (bf16[512,256]{1,0:T(8,128)(2,1)S(1)}, bf16[512,256]{1,0:T(8,128)(2,1)S(1)}, u32[]{:S(2)}, u32[]{:S(2)}) collective-permute-start(bf16[512,256]{1,0:T(8,128)(2,1)S(1)} %pad_maximum_fusion.1), channel_id=1, source_target_pairs={{24,0},{32,8},{40,16},{48,24},{56,32},{64,40},{72,48},{80,56},{88,... | collective-permute-start | bytes 786440 | tf_op jit(solution)/shard_map/ppermute | solution.py:15
  95.7 2.9 %copy-start.3 = (bf16[48,128,256]{2,1,0:T(8,128)(2,1)S(1)}, bf16[48,128,256]{2,1,0:T(8,128)(2,1)}, u32[]{:S(2)}) copy-start(bf16[48,128,256]{2,1,0:T(8,128)(2,1)} %gather_fusion.1) | copy-start | bytes 9437188
  95.7 3.3 %copy-start.6 = (bf16[4,12,128,128]{3,2,1,0:T(8,128)(2,1)S(1)}, bf16[4,12,128,128]{3,2,1,0:T(8,128)(2,1)}, u32[]{:S(2)}) copy-start(bf16[4,12,128,128]{3,2,1,0:T(8,128)(2,1)} %param.14) | copy-start | bytes 4718596
  100.1 20.1 %collective-permute-start.12 = (bf16[512,256]{1,0:T(8,128)(2,1)S(1)}, bf16[512,256]{1,0:T(8,128)(2,1)S(1)}, u32[]{:S(2)}, u32[]{:S(2)}) collective-permute-start(bf16[512,256]{1,0:T(8,128)(2,1)S(1)} %pad_maximum_fusion.2), channel_id=1, source_target_pairs={{0,24},{8,32},{16,40},{24,48},{32,56},{40,64},{48,72},{56,80},{64,... | collective-permute-start | bytes 786440 | tf_op jit(solution)/shard_map/ppermute | solution.py:15
  102.0 20.2 %collective-permute-start.13 = (bf16[512,256]{1,0:T(8,128)(2,1)S(1)}, bf16[512,256]{1,0:T(8,128)(2,1)S(1)}, u32[]{:S(2)}, u32[]{:S(2)}) collective-permute-start(bf16[512,256]{1,0:T(8,128)(2,1)S(1)} %pad_maximum_fusion.2), channel_id=1, source_target_pairs={{0,16},{8,24},{16,32},{24,40},{32,48},{40,56},{48,64},{56,72},{64,... | collective-permute-start | bytes 786440 | tf_op jit(solution)/shard_map/ppermute | solution.py:15
  107.8 18.8 %collective-permute-start.14 = (bf16[512,256]{1,0:T(8,128)(2,1)S(1)}, bf16[512,256]{1,0:T(8,128)(2,1)S(1)}, u32[]{:S(2)}, u32[]{:S(2)}) collective-permute-start(bf16[512,256]{1,0:T(8,128)(2,1)S(1)} %pad_maximum_fusion.2), channel_id=1, source_target_pairs={{0,8},{8,16},{16,24},{24,32},{32,40},{40,48},{48,56},{56,64},{64,7... | collective-permute-start | bytes 786440 | tf_op jit(solution)/shard_map/ppermute | solution.py:15
  111.3 15.4 %collective-permute-start.15 = (bf16[512,256]{1,0:T(8,128)(2,1)S(1)}, bf16[512,256]{1,0:T(8,128)(2,1)S(1)}, u32[]{:S(2)}, u32[]{:S(2)}) collective-permute-start(bf16[512,256]{1,0:T(8,128)(2,1)S(1)} %pad_maximum_fusion.2), channel_id=1, source_target_pairs={{8,0},{16,8},{24,16},{32,24},{40,32},{48,40},{56,48},{64,56},{72,6... | collective-permute-start | bytes 786440 | tf_op jit(solution)/shard_map/ppermute | solution.py:15
  116.8 17.4 %collective-permute-start.16 = (bf16[512,256]{1,0:T(8,128)(2,1)S(1)}, bf16[512,256]{1,0:T(8,128)(2,1)S(1)}, u32[]{:S(2)}, u32[]{:S(2)}) collective-permute-start(bf16[512,256]{1,0:T(8,128)(2,1)S(1)} %pad_maximum_fusion.2), channel_id=1, source_target_pairs={{16,0},{24,8},{32,16},{40,24},{48,32},{56,40},{64,48},{72,56},{80,... | collective-permute-start | bytes 786440 | tf_op jit(solution)/shard_map/ppermute | solution.py:15
  120.2 15.6 %collective-permute-start.17 = (bf16[512,256]{1,0:T(8,128)(2,1)S(1)}, bf16[512,256]{1,0:T(8,128)(2,1)S(1)}, u32[]{:S(2)}, u32[]{:S(2)}) collective-permute-start(bf16[512,256]{1,0:T(8,128)(2,1)S(1)} %pad_maximum_fusion.2), channel_id=1, source_target_pairs={{24,0},{32,8},{40,16},{48,24},{56,32},{64,40},{72,48},{80,56},{88,... | collective-permute-start | bytes 786440 | tf_op jit(solution)/shard_map/ppermute | solution.py:15
  138.3 2.9 %copy-start.1 = (bf16[48,128,256]{2,1,0:T(8,128)(2,1)S(1)}, bf16[48,128,256]{2,1,0:T(8,128)(2,1)}, u32[]{:S(2)}) copy-start(bf16[48,128,256]{2,1,0:T(8,128)(2,1)} %gather_fusion.2) | copy-start | bytes 9437188
  138.3 3.3 %copy-start.7 = (bf16[4,12,128,128]{3,2,1,0:T(8,128)(2,1)S(1)}, bf16[4,12,128,128]{3,2,1,0:T(8,128)(2,1)}, u32[]{:S(2)}) copy-start(bf16[4,12,128,128]{3,2,1,0:T(8,128)(2,1)} %param.14) | copy-start | bytes 4718596
where the time goes:
time: 171 us; the launch traced here: 170 us
  starting transfers between devices  68 us (40%)
  blocking collectives  25.8 us (15%)
  waiting for transfers between devices  25.7 us (15%)
  local copies, waits for them, and re-layouts  24.2 us (14%)
  other arithmetic  13.6 us (8%)
  matrix products  10.9 us (6%)
  between operations  1.72 us (1%)
    ppermute x18, starting transfers between devices, from_behind(): lax.ppermute(value, axis, [(source, source + steps) for source in range(l...  68 us
    psum x1, blocking collectives, shards(): scen_total = lax.psum(local_sum, 'scen')  25.8 us
    ppermute x18, waiting for transfers between devices, from_behind(): lax.ppermute(value, axis, [(source, source + steps) for source in range(l...  25.7 us
    unnamed x33, local copies, waits for them, and re-layouts  10.6 us
    gather x3, local copies, waits for them, and re-layouts, shards(): gathered = jnp.take(nearby, window_index, axis=0)  10.5 us
    dot_general x3, matrix products, shards(): jnp.einsum('bsij,bsjk->bik', impedance_real, gathered, preferred_element_...  8.52 us
    scatter-add x1, other arithmetic, shards(): jax.ops.segment_sum(both_power, local_phase, num_segments=phase_count)  6.25 us
  transfers between devices with their start and end apart: 18, of which 5 were waited for; matrix products, arithmetic and copies ran while one was open for 7% of the time, Pallas kernels for 0%

commit v1 on v0

--- a/solution.py
+++ b/solution.py
@@ -83,7 +83,11 @@
         volt_imag = source_imag - drop_imag
     magnitude = jnp.sqrt(volt_real * volt_real + volt_imag * volt_imag)
     local_sum = jnp.sum(magnitude.reshape(phase_count, local_scen, TIMES), axis=1)
-    scen_total = lax.psum(local_sum, "scen")
+    scen_total = local_sum
+    for hop in (1, 2, 4):
+        scen_total = scen_total + lax.ppermute(
+            scen_total, "scen", [(dev, dev ^ hop) for dev in range(8)]
+        )
     drop_mean = 100.0 * (1.0 - scen_total / total_scen)
     return (volt_real, volt_imag, drop_mean)
 

time: 171 us -> 162 us (0.947)
  the two profiles are of different devices: /device:TPU:224 before, /device:TPU:194 now
where the time goes in v1:
time: 162 us; the launch traced here: 161 us
  starting transfers between devices  76.6 us (47%)
  waiting for transfers between devices  33.8 us (21%)
  local copies, waits for them, and re-layouts  24.2 us (15%)
  other arithmetic  13.6 us (8%)
  matrix products  10.9 us (7%)
  between operations  1.75 us (1%)
    ppermute x18, starting transfers between devices, from_behind(): lax.ppermute(value, axis, [(source, source + steps) for source in range(l...  66.1 us
    ppermute x18, waiting for transfers between devices, from_behind(): lax.ppermute(value, axis, [(source, source + steps) for source in range(l...  28.1 us
    unnamed x33, local copies, waits for them, and re-layouts  10.6 us
    ppermute x3, starting transfers between devices, shards(): lax.ppermute(scen_total, 'scen', [(dev, dev ^ hop) for dev in range(8)])  10.5 us
    gather x3, local copies, waits for them, and re-layouts, shards(): gathered = jnp.take(nearby, window_index, axis=0)  10.5 us
    dot_general x3, matrix products, shards(): jnp.einsum('bsij,bsjk->bik', impedance_real, gathered, preferred_element_...  8.52 us
    scatter-add x1, other arithmetic, shards(): jax.ops.segment_sum(both_power, local_phase, num_segments=phase_count)  6.25 us
    ppermute x3, waiting for transfers between devices, shards(): lax.ppermute(scen_total, 'scen', [(dev, dev ^ hop) for dev in range(8)])  5.7 us
  transfers between devices with their start and end apart: 21, of which 9 were waited for; matrix products, arithmetic and copies ran while one was open for 8% of the time, Pallas kernels for 0%

profile of v1, /device:TPU:194, one launch (start us, length us, event | category | flops | bytes accessed | tf_op | source)
XLA Modules:
  0.0 160.8 jit_solution(3694248639321459320)
XLA Ops:
  0.7 0.8 fusion.42
  1.5 0.7 broadcast_subtract_fusion
  2.2 1.4 broadcast_multiply_fusion
  3.6 6.2 %scatter_custom_fusion = f32[512,256]{1,0:T(8,128)S(1)} fusion(s32[1024]{0:T(1024)S(1)} %broadcast_subtract_fusion, f32[1024,128]{1,0:T(8,128)S(1)} %get-tuple-element.12, f32[]{:T(128)} %constant.112, f32[1024,128]{1,0:T(8,128)S(1)} %get-tuple-element.13, f32[]{:T(128)} %constant.78.clone.1), kind=kCustom, calls=%fused_computation.7 | custom fusion | flops 524288 | bytes 1572872 | tf_op jit(solution)/shard_map/scatter-add | solution.py:44
  10.2 3.8 %collective-permute-start = (bf16[512,256]{1,0:T(8,128)(2,1)S(1)}, bf16[512,256]{1,0:T(8,128)(2,1)}, u32[]{:S(2)}, u32[]{:S(2)}) collective-permute-start(bf16[512,256]{1,0:T(8,128)(2,1)S(1)} %pad_maximum_fusion), channel_id=1, source_target_pairs={{0,24},{8,32},{16,40},{24,48},{32,56},{40,64},{48,72},{56,80},{64,... | collective-permute-start | bytes 786440 | tf_op jit(solution)/shard_map/ppermute | solution.py:15
  14.0 4.3 %collective-permute-start.1 = (bf16[512,256]{1,0:T(8,128)(2,1)S(1)}, bf16[512,256]{1,0:T(8,128)(2,1)}, u32[]{:S(2)}, u32[]{:S(2)}) collective-permute-start(bf16[512,256]{1,0:T(8,128)(2,1)S(1)} %pad_maximum_fusion), channel_id=1, source_target_pairs={{0,16},{8,24},{16,32},{24,40},{32,48},{40,56},{48,64},{56,72},{64,... | collective-permute-start | bytes 786440 | tf_op jit(solution)/shard_map/ppermute | solution.py:15
  18.3 3.7 %collective-permute-start.2 = (bf16[512,256]{1,0:T(8,128)(2,1)S(1)}, bf16[512,256]{1,0:T(8,128)(2,1)S(1)}, u32[]{:S(2)}, u32[]{:S(2)}) collective-permute-start(bf16[512,256]{1,0:T(8,128)(2,1)S(1)} %pad_maximum_fusion), channel_id=1, source_target_pairs={{0,8},{8,16},{16,24},{24,32},{32,40},{40,48},{48,56},{56,64},{64,7... | collective-permute-start | bytes 786440 | tf_op jit(solution)/shard_map/ppermute | solution.py:15
  22.0 2.1 %collective-permute-start.3 = (bf16[512,256]{1,0:T(8,128)(2,1)S(1)}, bf16[512,256]{1,0:T(8,128)(2,1)S(1)}, u32[]{:S(2)}, u32[]{:S(2)}) collective-permute-start(bf16[512,256]{1,0:T(8,128)(2,1)S(1)} %pad_maximum_fusion), channel_id=1, source_target_pairs={{8,0},{16,8},{24,16},{32,24},{40,32},{48,40},{56,48},{64,56},{72,6... | collective-permute-start | bytes 786440 | tf_op jit(solution)/shard_map/ppermute | solution.py:15
  24.2 4.0 %collective-permute-start.4 = (bf16[512,256]{1,0:T(8,128)(2,1)S(1)}, bf16[512,256]{1,0:T(8,128)(2,1)S(1)}, u32[]{:S(2)}, u32[]{:S(2)}) collective-permute-start(bf16[512,256]{1,0:T(8,128)(2,1)S(1)} %pad_maximum_fusion), channel_id=1, source_target_pairs={{16,0},{24,8},{32,16},{40,24},{48,32},{56,40},{64,48},{72,56},{80,... | collective-permute-start | bytes 786440 | tf_op jit(solution)/shard_map/ppermute | solution.py:15
  28.3 0.6 dynamic_slice.3
  28.9 1.3 fusion.27
  30.9 4.1 %collective-permute-start.5 = (bf16[512,256]{1,0:T(8,128)(2,1)S(1)}, bf16[512,256]{1,0:T(8,128)(2,1)S(1)}, u32[]{:S(2)}, u32[]{:S(2)}) collective-permute-start(bf16[512,256]{1,0:T(8,128)(2,1)S(1)} %pad_maximum_fusion), channel_id=1, source_target_pairs={{24,0},{32,8},{40,16},{48,24},{56,32},{64,40},{72,48},{80,56},{88,... | collective-permute-start | bytes 786440 | tf_op jit(solution)/shard_map/ppermute | solution.py:15
  34.9 1.7 %constant_dynamic-update-slice_fusion.6 = bf16[3584,256]{1,0:T(8,128)(2,1)} fusion(bf16[512,256]{1,0:T(8,128)(2,1)} %collective-permute-done), kind=kLoop, calls=%fused_computation.50 | loop fusion | bytes 524288
  36.6 1.7 %constant_dynamic-update-slice_fusion.5 = bf16[3584,256]{1,0:T(8,128)(2,1)} fusion(bf16[3584,256]{1,0:T(8,128)(2,1)} %constant_dynamic-update-slice_fusion.6, bf16[512,256]{1,0:T(8,128)(2,1)} %collective-permute-done.1), kind=kLoop, calls=%fused_computation.49 | loop fusion | bytes 524288
  38.3 0.7 constant_dynamic-update-slice_fusion.4
  39.0 0.7 constant_dynamic-update-slice_fusion.3
  39.7 0.7 constant_dynamic-update-slice_fusion.2
  40.5 0.7 constant_dynamic-update-slice_fusion.1
  41.2 6.1 %collective-permute-done.5 = bf16[512,256]{1,0:T(8,128)(2,1)S(1)} collective-permute-done((bf16[512,256]{1,0:T(8,128)(2,1)S(1)}, bf16[512,256]{1,0:T(8,128)(2,1)S(1)}, u32[]{:S(2)}, u32[]{:S(2)}) %collective-permute-start.5) | collective-permute-done | bytes 262176 | tf_op jit(solution)/shard_map/ppermute | solution.py:15
  47.3 0.7 constant_dynamic-update-slice_fusion
  48.0 4.0 %gather_fusion = bf16[48,128,256]{2,1,0:T(8,128)(2,1)} fusion(bf16[28,128,256]{2,1,0:T(8,128)(2,1)} %bitcast.1, s32[1024]{0:T(1024)S(1)} %pad_clamp_fusion), kind=kCustom, calls=%fused_computation.clone | custom fusion | bytes 6291648 | tf_op jit(solution)/shard_map/jit(_take)/gather | solution.py:72
  52.0 2.8 %fusion.4 = f32[4,256,128,1]{1,2,3,0:T(8,128)S(1)} fusion(bf16[4,12,128,128]{3,2,1,0:T(8,128)(2,1)S(1)} %copy-done, bf16[4,12,128,256]{3,2,1,0:T(8,128)(2,1)} %bitcast.53, pred[12]{0:T(512)(128)(4,1)S(1)} %iota_compare_fusion, pred[4,12]{1,0:T(4,128)(4,1)S(1)} %get-tuple-element.10), kind=kOutput, calls=%fused_computation.11 | convolution fusion | flops 405798912 | bytes 5242940 | tf_op jit(solution)/shard_map/bsij,bsjk->bik/dot_general | solution.py:74
  54.9 0.4 copy-done.5
  55.3 0.8 fusion.5
  56.4 2.4 %collective-permute-start.6 = (bf16[512,256]{1,0:T(8,128)(2,1)S(1)}, bf16[512,256]{1,0:T(8,128)(2,1)S(1)}, u32[]{:S(2)}, u32[]{:S(2)}) collective-permute-start(bf16[512,256]{1,0:T(8,128)(2,1)S(1)} %pad_maximum_fusion.1), channel_id=1, source_target_pairs={{0,24},{8,32},{16,40},{24,48},{32,56},{40,64},{48,72},{56,80},{64,... | collective-permute-start | bytes 786440 | tf_op jit(solution)/shard_map/ppermute | solution.py:15
  58.8 5.1 %collective-permute-start.7 = (bf16[512,256]{1,0:T(8,128)(2,1)S(1)}, bf16[512,256]{1,0:T(8,128)(2,1)S(1)}, u32[]{:S(2)}, u32[]{:S(2)}) collective-permute-start(bf16[512,256]{1,0:T(8,128)(2,1)S(1)} %pad_maximum_fusion.1), channel_id=1, source_target_pairs={{0,16},{8,24},{16,32},{24,40},{32,48},{40,56},{48,64},{56,72},{64,... | collective-permute-start | bytes 786440 | tf_op jit(solution)/shard_map/ppermute | solution.py:15
  63.9 1.9 %collective-permute-start.8 = (bf16[512,256]{1,0:T(8,128)(2,1)S(1)}, bf16[512,256]{1,0:T(8,128)(2,1)S(1)}, u32[]{:S(2)}, u32[]{:S(2)}) collective-permute-start(bf16[512,256]{1,0:T(8,128)(2,1)S(1)} %pad_maximum_fusion.1), channel_id=1, source_target_pairs={{0,8},{8,16},{16,24},{24,32},{32,40},{40,48},{48,56},{56,64},{64,7... | collective-permute-start | bytes 786440 | tf_op jit(solution)/shard_map/ppermute | solution.py:15
  65.8 3.9 %collective-permute-start.9 = (bf16[512,256]{1,0:T(8,128)(2,1)S(1)}, bf16[512,256]{1,0:T(8,128)(2,1)S(1)}, u32[]{:S(2)}, u32[]{:S(2)}) collective-permute-start(bf16[512,256]{1,0:T(8,128)(2,1)S(1)} %pad_maximum_fusion.1), channel_id=1, source_target_pairs={{8,0},{16,8},{24,16},{32,24},{40,32},{48,40},{56,48},{64,56},{72,6... | collective-permute-start | bytes 786440 | tf_op jit(solution)/shard_map/ppermute | solution.py:15
  69.8 4.4 %collective-permute-start.10 = (bf16[512,256]{1,0:T(8,128)(2,1)S(1)}, bf16[512,256]{1,0:T(8,128)(2,1)S(1)}, u32[]{:S(2)}, u32[]{:S(2)}) collective-permute-start(bf16[512,256]{1,0:T(8,128)(2,1)S(1)} %pad_maximum_fusion.1), channel_id=1, source_target_pairs={{16,0},{24,8},{32,16},{40,24},{48,32},{56,40},{64,48},{72,56},{80,... | collective-permute-start | bytes 786440 | tf_op jit(solution)/shard_map/ppermute | solution.py:15
  74.1 4.3 %collective-permute-start.11 = (bf16[512,256]{1,0:T(8,128)(2,1)S(1)}, bf16[512,256]{1,0:T(8,128)(2,1)S(1)}, u32[]{:S(2)}, u32[]{:S(2)}) collective-permute-start(bf16[512,256]{1,0:T(8,128)(2,1)S(1)} %pad_maximum_fusion.1), channel_id=1, source_target_pairs={{24,0},{32,8},{40,16},{48,24},{56,32},{64,40},{72,48},{80,56},{88,... | collective-permute-start | bytes 786440 | tf_op jit(solution)/shard_map/ppermute | solution.py:15
  78.5 0.7 constant_dynamic-update-slice_fusion.13
  79.2 0.7 constant_dynamic-update-slice_fusion.12
  80.0 0.7 constant_dynamic-update-slice_fusion.11
  80.7 0.7 constant_dynamic-update-slice_fusion.10
  81.4 0.7 constant_dynamic-update-slice_fusion.9
  82.1 2.9 %collective-permute-done.10 = bf16[512,256]{1,0:T(8,128)(2,1)S(1)} collective-permute-done((bf16[512,256]{1,0:T(8,128)(2,1)S(1)}, bf16[512,256]{1,0:T(8,128)(2,1)S(1)}, u32[]{:S(2)}, u32[]{:S(2)}) %collective-permute-start.10) | collective-permute-done | bytes 262176 | tf_op jit(solution)/shard_map/ppermute | solution.py:15
  85.1 0.7 constant_dynamic-update-slice_fusion.8
  85.8 7.0 %collective-permute-done.11 = bf16[512,256]{1,0:T(8,128)(2,1)S(1)} collective-permute-done((bf16[512,256]{1,0:T(8,128)(2,1)S(1)}, bf16[512,256]{1,0:T(8,128)(2,1)S(1)}, u32[]{:S(2)}, u32[]{:S(2)}) %collective-permute-start.11) | collective-permute-done | bytes 262176 | tf_op jit(solution)/shard_map/ppermute | solution.py:15
  92.8 0.7 constant_dynamic-update-slice_fusion.7
  93.6 4.0 %gather_fusion.1 = bf16[48,128,256]{2,1,0:T(8,128)(2,1)} fusion(bf16[28,128,256]{2,1,0:T(8,128)(2,1)} %bitcast.15, s32[1024]{0:T(1024)S(1)} %pad_clamp_fusion), kind=kCustom, calls=%fused_computation.1.clone | custom fusion | bytes 6291648 | tf_op jit(solution)/shard_map/jit(_take)/gather | solution.py:72
  97.5 2.8 %fusion.6 = f32[4,256,128,1]{1,2,3,0:T(8,128)S(1)} fusion(bf16[4,12,128,128]{3,2,1,0:T(8,128)(2,1)S(1)} %copy-done, bf16[4,12,128,256]{3,2,1,0:T(8,128)(2,1)} %bitcast.55, pred[12]{0:T(512)(128)(4,1)S(1)} %iota_compare_fusion, pred[4,12]{1,0:T(4,128)(4,1)S(1)} %get-tuple-element.10), kind=kOutput, calls=%fused_computation.13 | convolution fusion | flops 405798912 | bytes 5242940 | tf_op jit(solution)/shard_map/bsij,bsjk->bik/dot_general | solution.py:74
  100.4 0.4 copy-done.6
  100.8 0.8 fusion.7
  101.9 1.9 %collective-permute-start.12 = (bf16[512,256]{1,0:T(8,128)(2,1)S(1)}, bf16[512,256]{1,0:T(8,128)(2,1)S(1)}, u32[]{:S(2)}, u32[]{:S(2)}) collective-permute-start(bf16[512,256]{1,0:T(8,128)(2,1)S(1)} %pad_maximum_fusion.2), channel_id=1, source_target_pairs={{0,24},{8,32},{16,40},{24,48},{32,56},{40,64},{48,72},{56,80},{64,... | collective-permute-start | bytes 786440 | tf_op jit(solution)/shard_map/ppermute | solution.py:15
  103.9 3.6 %collective-permute-start.13 = (bf16[512,256]{1,0:T(8,128)(2,1)S(1)}, bf16[512,256]{1,0:T(8,128)(2,1)S(1)}, u32[]{:S(2)}, u32[]{:S(2)}) collective-permute-start(bf16[512,256]{1,0:T(8,128)(2,1)S(1)} %pad_maximum_fusion.2), channel_id=1, source_target_pairs={{0,16},{8,24},{16,32},{24,40},{32,48},{40,56},{48,64},{56,72},{64,... | collective-permute-start | bytes 786440 | tf_op jit(solution)/shard_map/ppermute | solution.py:15
  107.5 1.9 %collective-permute-start.14 = (bf16[512,256]{1,0:T(8,128)(2,1)S(1)}, bf16[512,256]{1,0:T(8,128)(2,1)S(1)}, u32[]{:S(2)}, u32[]{:S(2)}) collective-permute-start(bf16[512,256]{1,0:T(8,128)(2,1)S(1)} %pad_maximum_fusion.2), channel_id=1, source_target_pairs={{0,8},{8,16},{16,24},{24,32},{32,40},{40,48},{48,56},{56,64},{64,7... | collective-permute-start | bytes 786440 | tf_op jit(solution)/shard_map/ppermute | solution.py:15
  109.4 3.9 %collective-permute-start.15 = (bf16[512,256]{1,0:T(8,128)(2,1)S(1)}, bf16[512,256]{1,0:T(8,128)(2,1)S(1)}, u32[]{:S(2)}, u32[]{:S(2)}) collective-permute-start(bf16[512,256]{1,0:T(8,128)(2,1)S(1)} %pad_maximum_fusion.2), channel_id=1, source_target_pairs={{8,0},{16,8},{24,16},{32,24},{40,32},{48,40},{56,48},{64,56},{72,6... | collective-permute-start | bytes 786440 | tf_op jit(solution)/shard_map/ppermute | solution.py:15
  113.3 4.6 %collective-permute-start.16 = (bf16[512,256]{1,0:T(8,128)(2,1)S(1)}, bf16[512,256]{1,0:T(8,128)(2,1)S(1)}, u32[]{:S(2)}, u32[]{:S(2)}) collective-permute-start(bf16[512,256]{1,0:T(8,128)(2,1)S(1)} %pad_maximum_fusion.2), channel_id=1, source_target_pairs={{16,0},{24,8},{32,16},{40,24},{48,32},{56,40},{64,48},{72,56},{80,... | collective-permute-start | bytes 786440 | tf_op jit(solution)/shard_map/ppermute | solution.py:15
  118.0 6.0 %collective-permute-start.17 = (bf16[512,256]{1,0:T(8,128)(2,1)S(1)}, bf16[512,256]{1,0:T(8,128)(2,1)S(1)}, u32[]{:S(2)}, u32[]{:S(2)}) collective-permute-start(bf16[512,256]{1,0:T(8,128)(2,1)S(1)} %pad_maximum_fusion.2), channel_id=1, source_target_pairs={{24,0},{32,8},{40,16},{48,24},{56,32},{64,40},{72,48},{80,56},{88,... | collective-permute-start | bytes 786440 | tf_op jit(solution)/shard_map/ppermute | solution.py:15
  124.2 1.2 collective-permute-done.15
  125.4 4.2 %collective-permute-done.16 = bf16[512,256]{1,0:T(8,128)(2,1)S(1)} collective-permute-done((bf16[512,256]{1,0:T(8,128)(2,1)S(1)}, bf16[512,256]{1,0:T(8,128)(2,1)S(1)}, u32[]{:S(2)}, u32[]{:S(2)}) %collective-permute-start.16) | collective-permute-done | bytes 262176 | tf_op jit(solution)/shard_map/ppermute | solution.py:15
  129.6 6.6 %collective-permute-done.17 = bf16[512,256]{1,0:T(8,128)(2,1)S(1)} collective-permute-done((bf16[512,256]{1,0:T(8,128)(2,1)S(1)}, bf16[512,256]{1,0:T(8,128)(2,1)S(1)}, u32[]{:S(2)}, u32[]{:S(2)}) %collective-permute-start.17) | collective-permute-done | bytes 262176 | tf_op jit(solution)/shard_map/ppermute | solution.py:15
  136.2 2.5 %gather_fusion.2 = bf16[48,128,256]{2,1,0:T(8,128)(2,1)} fusion(bf16[28,128,256]{2,1,0:T(8,128)(2,1)S(1)} %bitcast.50, s32[1024]{0:T(1024)S(1)} %pad_clamp_fusion), kind=kCustom, calls=%fused_computation.2.clone | custom fusion | bytes 6291648 | tf_op jit(solution)/shard_map/jit(_take)/gather | solution.py:72
  138.7 2.8 %fusion.8 = f32[4,256,128,1]{1,2,3,0:T(8,128)S(1)} fusion(bf16[4,12,128,128]{3,2,1,0:T(8,128)(2,1)S(1)} %copy-done, bf16[4,12,128,256]{3,2,1,0:T(8,128)(2,1)} %bitcast.51, pred[12]{0:T(512)(128)(4,1)S(1)} %iota_compare_fusion, pred[4,12]{1,0:T(4,128)(4,1)S(1)} %get-tuple-element.10), kind=kOutput, calls=%fused_computation.15 | convolution fusion | flops 405798912 | bytes 5242940 | tf_op jit(solution)/shard_map/bsij,bsjk->bik/dot_general | solution.py:74
  141.6 0.4 copy-done.7
  142.0 0.8 fusion.9
  142.8 1.0 add_sqrt_fusion
  144.0 1.9 %collective-permute-start.18 = (f32[512,16]{0,1:T(8,128)S(1)}, f32[512,16]{0,1:T(8,128)S(1)}, u32[]{:S(2)}, u32[]{:S(2)}) collective-permute-start(f32[512,16]{0,1:T(8,128)S(1)} %reduce_sum.19), channel_id=1, source_target_pairs={{0,1},{1,0},{2,3},{3,2},{4,5},{5,4},{6,7},{7,6},{8,9},{9,8},{10,11... | collective-permute-start | bytes 98312 | tf_op jit(solution)/shard_map/ppermute | solution.py:88
  145.9 1.2 collective-permute-done.18
  147.1 3.5 %collective-permute-start.19 = (f32[512,16]{0,1:T(8,128)S(1)}, f32[512,16]{0,1:T(8,128)S(1)}, u32[]{:S(2)}, u32[]{:S(2)}) collective-permute-start(f32[512,16]{0,1:T(8,128)S(1)} %add.109), channel_id=1, source_target_pairs={{0,2},{1,3},{2,0},{3,1},{4,6},{5,7},{6,4},{7,5},{8,10},{9,11},{10,... | collective-permute-start | bytes 98312 | tf_op jit(solution)/shard_map/ppermute | solution.py:88
  150.6 2.3 %collective-permute-done.19 = f32[512,16]{0,1:T(8,128)S(1)} collective-permute-done((f32[512,16]{0,1:T(8,128)S(1)}, f32[512,16]{0,1:T(8,128)S(1)}, u32[]{:S(2)}, u32[]{:S(2)}) %collective-permute-start.19) | collective-permute-done | bytes 32800 | tf_op jit(solution)/shard_map/ppermute | solution.py:88
  152.9 5.1 %collective-permute-start.20 = (f32[512,16]{0,1:T(8,128)S(1)}, f32[512,16]{0,1:T(8,128)S(1)}, u32[]{:S(2)}, u32[]{:S(2)}) collective-permute-start(f32[512,16]{0,1:T(8,128)S(1)} %add.110), channel_id=1, source_target_pairs={{0,4},{1,5},{2,6},{3,7},{4,0},{5,1},{6,2},{7,3},{8,12},{9,13},{10,... | collective-permute-start | bytes 98312 | tf_op jit(solution)/shard_map/ppermute | solution.py:88
  158.0 2.2 %collective-permute-done.20 = f32[512,16]{0,1:T(8,128)S(1)} collective-permute-done((f32[512,16]{0,1:T(8,128)S(1)}, f32[512,16]{0,1:T(8,128)S(1)}, u32[]{:S(2)}, u32[]{:S(2)}) %collective-permute-start.20) | collective-permute-done | bytes 32800 | tf_op jit(solution)/shard_map/ppermute | solution.py:88
  160.2 0.6 subtract_multiply_fusion
  (50 shorter events, 1.4 us)
Async XLA Ops:
  0.6 51.4 %copy-start = (bf16[4,12,128,128]{3,2,1,0:T(8,128)(2,1)S(1)}, bf16[4,12,128,128]{3,2,1,0:T(8,128)(2,1)}, u32[]{:S(2)}) copy-start(bf16[4,12,128,128]{3,2,1,0:T(8,128)(2,1)} %param.13) | copy-start | bytes 4718596
  3.6 24.6 %copy-start.4 = (s32[4,12]{1,0:T(4,128)S(1)}, s32[4,12]{1,0:T(4,128)}, u32[]{:S(2)}) copy-start(s32[4,12]{1,0:T(4,128)} %param.12) | copy-start | bytes 580
  3.6 24.7 %copy-start.8 = (s32[64]{0:T(128)S(1)}, s32[64]{0:T(128)}, u32[]{:S(2)}) copy-start(s32[64]{0:T(128)} %param.11) | copy-start | bytes 772
  10.2 20.7 %collective-permute-start = (bf16[512,256]{1,0:T(8,128)(2,1)S(1)}, bf16[512,256]{1,0:T(8,128)(2,1)}, u32[]{:S(2)}, u32[]{:S(2)}) collective-permute-start(bf16[512,256]{1,0:T(8,128)(2,1)S(1)} %pad_maximum_fusion), channel_id=1, source_target_pairs={{0,24},{8,32},{16,40},{24,48},{32,56},{40,64},{48,72},{56,80},{64,... | collective-permute-start | bytes 786440 | tf_op jit(solution)/shard_map/ppermute | solution.py:15
  14.0 22.6 %collective-permute-start.1 = (bf16[512,256]{1,0:T(8,128)(2,1)S(1)}, bf16[512,256]{1,0:T(8,128)(2,1)}, u32[]{:S(2)}, u32[]{:S(2)}) collective-permute-start(bf16[512,256]{1,0:T(8,128)(2,1)S(1)} %pad_maximum_fusion), channel_id=1, source_target_pairs={{0,16},{8,24},{16,32},{24,40},{32,48},{40,56},{48,64},{56,72},{64,... | collective-permute-start | bytes 786440 | tf_op jit(solution)/shard_map/ppermute | solution.py:15
  18.3 20.0 %collective-permute-start.2 = (bf16[512,256]{1,0:T(8,128)(2,1)S(1)}, bf16[512,256]{1,0:T(8,128)(2,1)S(1)}, u32[]{:S(2)}, u32[]{:S(2)}) collective-permute-start(bf16[512,256]{1,0:T(8,128)(2,1)S(1)} %pad_maximum_fusion), channel_id=1, source_target_pairs={{0,8},{8,16},{16,24},{24,32},{32,40},{40,48},{48,56},{56,64},{64,7... | collective-permute-start | bytes 786440 | tf_op jit(solution)/shard_map/ppermute | solution.py:15
  22.0 17.7 %collective-permute-start.3 = (bf16[512,256]{1,0:T(8,128)(2,1)S(1)}, bf16[512,256]{1,0:T(8,128)(2,1)S(1)}, u32[]{:S(2)}, u32[]{:S(2)}) collective-permute-start(bf16[512,256]{1,0:T(8,128)(2,1)S(1)} %pad_maximum_fusion), channel_id=1, source_target_pairs={{8,0},{16,8},{24,16},{32,24},{40,32},{48,40},{56,48},{64,56},{72,6... | collective-permute-start | bytes 786440 | tf_op jit(solution)/shard_map/ppermute | solution.py:15
  24.2 16.3 %collective-permute-start.4 = (bf16[512,256]{1,0:T(8,128)(2,1)S(1)}, bf16[512,256]{1,0:T(8,128)(2,1)S(1)}, u32[]{:S(2)}, u32[]{:S(2)}) collective-permute-start(bf16[512,256]{1,0:T(8,128)(2,1)S(1)} %pad_maximum_fusion), channel_id=1, source_target_pairs={{16,0},{24,8},{32,16},{40,24},{48,32},{56,40},{64,48},{72,56},{80,... | collective-permute-start | bytes 786440 | tf_op jit(solution)/shard_map/ppermute | solution.py:15
  30.9 16.4 %collective-permute-start.5 = (bf16[512,256]{1,0:T(8,128)(2,1)S(1)}, bf16[512,256]{1,0:T(8,128)(2,1)S(1)}, u32[]{:S(2)}, u32[]{:S(2)}) collective-permute-start(bf16[512,256]{1,0:T(8,128)(2,1)S(1)} %pad_maximum_fusion), channel_id=1, source_target_pairs={{24,0},{32,8},{40,16},{48,24},{56,32},{64,40},{72,48},{80,56},{88,... | collective-permute-start | bytes 786440 | tf_op jit(solution)/shard_map/ppermute | solution.py:15
  52.0 2.9 %copy-start.2 = (bf16[48,128,256]{2,1,0:T(8,128)(2,1)S(1)}, bf16[48,128,256]{2,1,0:T(8,128)(2,1)}, u32[]{:S(2)}) copy-start(bf16[48,128,256]{2,1,0:T(8,128)(2,1)} %gather_fusion) | copy-start | bytes 9437188
  52.0 3.3 %copy-start.5 = (bf16[4,12,128,128]{3,2,1,0:T(8,128)(2,1)S(1)}, bf16[4,12,128,128]{3,2,1,0:T(8,128)(2,1)}, u32[]{:S(2)}) copy-start(bf16[4,12,128,128]{3,2,1,0:T(8,128)(2,1)} %param.14) | copy-start | bytes 4718596
  56.4 17.8 %collective-permute-start.6 = (bf16[512,256]{1,0:T(8,128)(2,1)S(1)}, bf16[512,256]{1,0:T(8,128)(2,1)S(1)}, u32[]{:S(2)}, u32[]{:S(2)}) collective-permute-start(bf16[512,256]{1,0:T(8,128)(2,1)S(1)} %pad_maximum_fusion.1), channel_id=1, source_target_pairs={{0,24},{8,32},{16,40},{24,48},{32,56},{40,64},{48,72},{56,80},{64,... | collective-permute-start | bytes 786440 | tf_op jit(solution)/shard_map/ppermute | solution.py:15
  58.8 20.4 %collective-permute-start.7 = (bf16[512,256]{1,0:T(8,128)(2,1)S(1)}, bf16[512,256]{1,0:T(8,128)(2,1)S(1)}, u32[]{:S(2)}, u32[]{:S(2)}) collective-permute-start(bf16[512,256]{1,0:T(8,128)(2,1)S(1)} %pad_maximum_fusion.1), channel_id=1, source_target_pairs={{0,16},{8,24},{16,32},{24,40},{32,48},{40,56},{48,64},{56,72},{64,... | collective-permute-start | bytes 786440 | tf_op jit(solution)/shard_map/ppermute | solution.py:15
  63.9 16.0 %collective-permute-start.8 = (bf16[512,256]{1,0:T(8,128)(2,1)S(1)}, bf16[512,256]{1,0:T(8,128)(2,1)S(1)}, u32[]{:S(2)}, u32[]{:S(2)}) collective-permute-start(bf16[512,256]{1,0:T(8,128)(2,1)S(1)} %pad_maximum_fusion.1), channel_id=1, source_target_pairs={{0,8},{8,16},{16,24},{24,32},{32,40},{40,48},{48,56},{56,64},{64,7... | collective-permute-start | bytes 786440 | tf_op jit(solution)/shard_map/ppermute | solution.py:15
  65.8 15.6 %collective-permute-start.9 = (bf16[512,256]{1,0:T(8,128)(2,1)S(1)}, bf16[512,256]{1,0:T(8,128)(2,1)S(1)}, u32[]{:S(2)}, u32[]{:S(2)}) collective-permute-start(bf16[512,256]{1,0:T(8,128)(2,1)S(1)} %pad_maximum_fusion.1), channel_id=1, source_target_pairs={{8,0},{16,8},{24,16},{32,24},{40,32},{48,40},{56,48},{64,56},{72,6... | collective-permute-start | bytes 786440 | tf_op jit(solution)/shard_map/ppermute | solution.py:15
  69.8 15.3 %collective-permute-start.10 = (bf16[512,256]{1,0:T(8,128)(2,1)S(1)}, bf16[512,256]{1,0:T(8,128)(2,1)S(1)}, u32[]{:S(2)}, u32[]{:S(2)}) collective-permute-start(bf16[512,256]{1,0:T(8,128)(2,1)S(1)} %pad_maximum_fusion.1), channel_id=1, source_target_pairs={{16,0},{24,8},{32,16},{40,24},{48,32},{56,40},{64,48},{72,56},{80,... | collective-permute-start | bytes 786440 | tf_op jit(solution)/shard_map/ppermute | solution.py:15
  74.1 18.7 %collective-permute-start.11 = (bf16[512,256]{1,0:T(8,128)(2,1)S(1)}, bf16[512,256]{1,0:T(8,128)(2,1)S(1)}, u32[]{:S(2)}, u32[]{:S(2)}) collective-permute-start(bf16[512,256]{1,0:T(8,128)(2,1)S(1)} %pad_maximum_fusion.1), channel_id=1, source_target_pairs={{24,0},{32,8},{40,16},{48,24},{56,32},{64,40},{72,48},{80,56},{88,... | collective-permute-start | bytes 786440 | tf_op jit(solution)/shard_map/ppermute | solution.py:15
  97.5 2.9 %copy-start.3 = (bf16[48,128,256]{2,1,0:T(8,128)(2,1)S(1)}, bf16[48,128,256]{2,1,0:T(8,128)(2,1)}, u32[]{:S(2)}) copy-start(bf16[48,128,256]{2,1,0:T(8,128)(2,1)} %gather_fusion.1) | copy-start | bytes 9437188
  97.5 3.3 %copy-start.6 = (bf16[4,12,128,128]{3,2,1,0:T(8,128)(2,1)S(1)}, bf16[4,12,128,128]{3,2,1,0:T(8,128)(2,1)}, u32[]{:S(2)}) copy-start(bf16[4,12,128,128]{3,2,1,0:T(8,128)(2,1)} %param.14) | copy-start | bytes 4718596
  101.9 16.1 %collective-permute-start.12 = (bf16[512,256]{1,0:T(8,128)(2,1)S(1)}, bf16[512,256]{1,0:T(8,128)(2,1)S(1)}, u32[]{:S(2)}, u32[]{:S(2)}) collective-permute-start(bf16[512,256]{1,0:T(8,128)(2,1)S(1)} %pad_maximum_fusion.2), channel_id=1, source_target_pairs={{0,24},{8,32},{16,40},{24,48},{32,56},{40,64},{48,72},{56,80},{64,... | collective-permute-start | bytes 786440 | tf_op jit(solution)/shard_map/ppermute | solution.py:15
  103.9 20.2 %collective-permute-start.13 = (bf16[512,256]{1,0:T(8,128)(2,1)S(1)}, bf16[512,256]{1,0:T(8,128)(2,1)S(1)}, u32[]{:S(2)}, u32[]{:S(2)}) collective-permute-start(bf16[512,256]{1,0:T(8,128)(2,1)S(1)} %pad_maximum_fusion.2), channel_id=1, source_target_pairs={{0,16},{8,24},{16,32},{24,40},{32,48},{40,56},{48,64},{56,72},{64,... | collective-permute-start | bytes 786440 | tf_op jit(solution)/shard_map/ppermute | solution.py:15
  107.5 16.6 %collective-permute-start.14 = (bf16[512,256]{1,0:T(8,128)(2,1)S(1)}, bf16[512,256]{1,0:T(8,128)(2,1)S(1)}, u32[]{:S(2)}, u32[]{:S(2)}) collective-permute-start(bf16[512,256]{1,0:T(8,128)(2,1)S(1)} %pad_maximum_fusion.2), channel_id=1, source_target_pairs={{0,8},{8,16},{16,24},{24,32},{32,40},{40,48},{48,56},{56,64},{64,7... | collective-permute-start | bytes 786440 | tf_op jit(solution)/shard_map/ppermute | solution.py:15
  109.4 16.0 %collective-permute-start.15 = (bf16[512,256]{1,0:T(8,128)(2,1)S(1)}, bf16[512,256]{1,0:T(8,128)(2,1)S(1)}, u32[]{:S(2)}, u32[]{:S(2)}) collective-permute-start(bf16[512,256]{1,0:T(8,128)(2,1)S(1)} %pad_maximum_fusion.2), channel_id=1, source_target_pairs={{8,0},{16,8},{24,16},{32,24},{40,32},{48,40},{56,48},{64,56},{72,6... | collective-permute-start | bytes 786440 | tf_op jit(solution)/shard_map/ppermute | solution.py:15
  113.3 16.2 %collective-permute-start.16 = (bf16[512,256]{1,0:T(8,128)(2,1)S(1)}, bf16[512,256]{1,0:T(8,128)(2,1)S(1)}, u32[]{:S(2)}, u32[]{:S(2)}) collective-permute-start(bf16[512,256]{1,0:T(8,128)(2,1)S(1)} %pad_maximum_fusion.2), channel_id=1, source_target_pairs={{16,0},{24,8},{32,16},{40,24},{48,32},{56,40},{64,48},{72,56},{80,... | collective-permute-start | bytes 786440 | tf_op jit(solution)/shard_map/ppermute | solution.py:15
  118.0 18.2 %collective-permute-start.17 = (bf16[512,256]{1,0:T(8,128)(2,1)S(1)}, bf16[512,256]{1,0:T(8,128)(2,1)S(1)}, u32[]{:S(2)}, u32[]{:S(2)}) collective-permute-start(bf16[512,256]{1,0:T(8,128)(2,1)S(1)} %pad_maximum_fusion.2), channel_id=1, source_target_pairs={{24,0},{32,8},{40,16},{48,24},{56,32},{64,40},{72,48},{80,56},{88,... | collective-permute-start | bytes 786440 | tf_op jit(solution)/shard_map/ppermute | solution.py:15
  138.7 2.9 %copy-start.1 = (bf16[48,128,256]{2,1,0:T(8,128)(2,1)S(1)}, bf16[48,128,256]{2,1,0:T(8,128)(2,1)}, u32[]{:S(2)}) copy-start(bf16[48,128,256]{2,1,0:T(8,128)(2,1)} %gather_fusion.2) | copy-start | bytes 9437188
  138.7 3.3 %copy-start.7 = (bf16[4,12,128,128]{3,2,1,0:T(8,128)(2,1)S(1)}, bf16[4,12,128,128]{3,2,1,0:T(8,128)(2,1)}, u32[]{:S(2)}) copy-start(bf16[4,12,128,128]{3,2,1,0:T(8,128)(2,1)} %param.14) | copy-start | bytes 4718596
  144.0 3.1 %collective-permute-start.18 = (f32[512,16]{0,1:T(8,128)S(1)}, f32[512,16]{0,1:T(8,128)S(1)}, u32[]{:S(2)}, u32[]{:S(2)}) collective-permute-start(f32[512,16]{0,1:T(8,128)S(1)} %reduce_sum.19), channel_id=1, source_target_pairs={{0,1},{1,0},{2,3},{3,2},{4,5},{5,4},{6,7},{7,6},{8,9},{9,8},{10,11... | collective-permute-start | bytes 98312 | tf_op jit(solution)/shard_map/ppermute | solution.py:88
  147.1 5.8 %collective-permute-start.19 = (f32[512,16]{0,1:T(8,128)S(1)}, f32[512,16]{0,1:T(8,128)S(1)}, u32[]{:S(2)}, u32[]{:S(2)}) collective-permute-start(f32[512,16]{0,1:T(8,128)S(1)} %add.109), channel_id=1, source_target_pairs={{0,2},{1,3},{2,0},{3,1},{4,6},{5,7},{6,4},{7,5},{8,10},{9,11},{10,... | collective-permute-start | bytes 98312 | tf_op jit(solution)/shard_map/ppermute | solution.py:88
  152.9 7.3 %collective-permute-start.20 = (f32[512,16]{0,1:T(8,128)S(1)}, f32[512,16]{0,1:T(8,128)S(1)}, u32[]{:S(2)}, u32[]{:S(2)}) collective-permute-start(f32[512,16]{0,1:T(8,128)S(1)} %add.110), channel_id=1, source_target_pairs={{0,4},{1,5},{2,6},{3,7},{4,0},{5,1},{6,2},{7,3},{8,12},{9,13},{10,... | collective-permute-start | bytes 98312 | tf_op jit(solution)/shard_map/ppermute | solution.py:88
